TPU v7x, 256 devices: a whole 4x4x8 slice. The times are simulated.
256 devices in a mesh: dp: 8 (over x, z_lo), ctx: 32 (over y, z_hi, core).
Axes of the slice: x: 4, y: 4, z: 8 (z_hi: 4, z_lo: 2; z = z_hi * 2 + z_lo), core: 2. Of those that a mesh axis runs over, the one named last changes fastest.
Arguments:
- queries: bfloat16 [32768, 8192], P(('dp', 'ctx')), may hold values from -16 to 16
- out_grad: bfloat16 [32768, 8192], P(('dp', 'ctx')), may hold values from -6 to 6
- enc_states: bfloat16 [3072, 1024], P(('dp', 'ctx')), may hold values from -8 to 8
- w_key: bfloat16 [1024, 8192], P('dp', 'ctx'), may hold values from -1 to 1
- w_value: bfloat16 [1024, 8192], P('dp', 'ctx'), may hold values from -0.1875 to 0.1875
- dec_segments: int32 [32768], P(('dp', 'ctx')), may hold values from 0 to 3, as said below
- enc_segments: int32 [3072], P(('dp', 'ctx')), may hold values from 0 to 3, as said below
Outputs:
- query_grad: bfloat16 [32768, 8192], P(('dp', 'ctx'))
- enc_grad: bfloat16 [3072, 1024], P(('dp', 'ctx'))
- w_key_grad: float32 [1024, 8192], P('dp', 'ctx')
- w_value_grad: float32 [1024, 8192], P('dp', 'ctx')
Inputs may be any that keep to these rules, and one draw needn't show every extreme that they name: `dec_segments`: within each pack the ids never fall along the tokens, and each of the 4 ids has one or more decoder tokens in the pack. `enc_segments`: within each pack the ids never fall along the tokens, and each of the 4 ids has two or more encoder tokens in the pack.
All inputs are finite; a program needn't handle non-finite values.
Results may differ from a plain program's by a relative error of at most 0.019.
Values may be sent and summed in bfloat16 or wider, within the bound.
No kernel may reach another device: no remote copies, remote signals or barrier semaphores. Data moves between devices by JAX's collectives and lax.ppermute only.
A program may use at most 64 MiB of HBM per device.

v0:
```python
import math
import jax
import jax.numpy as jnp
from jax import lax
from jax.sharding import PartitionSpec as P

HEAD_DIM = 128


def side_by_side(arrays, axis, dim, along):
    ends, at = ([], 0)
    for a in arrays[:-1]:
        at += a.shape[along]
        ends.append(at)
    both = jnp.concatenate(arrays, axis=along)
    return tuple(jnp.split(lax.all_gather(both, axis, axis=dim, tiled=True), ends, axis=along))


def sent_to_all(value, axis):
    size = lax.axis_size(axis)
    return lax.all_to_all(
        jnp.broadcast_to(value[None], (size, *value.shape)), axis, 0, 0, tiled=True
    )


def joined_along(pieces, dim):
    pieces = jnp.moveaxis(pieces, 0, dim)
    lengths = pieces.shape
    return pieces.reshape(*lengths[:dim], lengths[dim] * lengths[dim + 1], *lengths[dim + 2 :])


def gathered_copies(value, axis, dim):
    pieces = sent_to_all(value, axis)
    return joined_along(pieces, dim)


def split_up(value, dim, size):
    lengths = value.shape
    pieces = value.reshape(*lengths[:dim], size, lengths[dim] // size, *lengths[dim + 1 :])
    return jnp.moveaxis(pieces, dim, 0)


def sum_at_owner(value, axis, dim):
    pieces = split_up(value, dim, lax.axis_size(axis))
    arrived = lax.all_to_all(pieces, axis, split_axis=0, concat_axis=0, tiled=True)
    return arrived.astype(jnp.float32).sum(axis=0)


def in_one_piece(arrays, axis, dim, along):
    ends, at = ([], 0)
    for a in arrays[:-1]:
        at += a.shape[along]
        ends.append(at)
    both = jnp.concatenate(arrays, axis=along)
    return tuple(
        jnp.split(lax.psum_scatter(both, axis, scatter_dimension=dim, tiled=True), ends, axis=along)
    )


def attend(queries, out_grads, key_rows, value_rows, query_ids, key_ids):
    length, full_width = queries.shape
    key_count = key_rows.shape[0]
    head_count = full_width // HEAD_DIM
    group_size = min(head_count, 16)
    column_count = group_size * HEAD_DIM
    row_count = math.gcd(length, 1024)

    def head_group(number):
        column_start = number * column_count
        key_block = key_rows.reshape(key_count, group_size, HEAD_DIM)
        value_block = value_rows.reshape(key_count, group_size, HEAD_DIM)

        def query_block(totals, block_number):
            first_row = block_number * row_count
            query_part = lax.dynamic_slice(
                queries, (first_row, column_start), (row_count, column_count)
            ).reshape(row_count, group_size, HEAD_DIM)
            grad_part = lax.dynamic_slice(
                out_grads, (first_row, column_start), (row_count, column_count)
            ).reshape(row_count, group_size, HEAD_DIM)
            block_ids = lax.dynamic_slice_in_dim(query_ids, first_row, row_count, 0)
            allowed = block_ids[:, None] == key_ids[None, :]
            scores = jnp.einsum(
                "qhd,khd->hqk", query_part, key_block, preferred_element_type=jnp.float32
            )
            scores = jnp.where(allowed[None], scores, -jnp.inf)
            highest = jnp.max(scores, axis=2, keepdims=True)
            weights = jnp.exp(scores - highest)
            probability = weights / jnp.sum(weights, axis=2, keepdims=True)
            upstream = jnp.einsum(
                "qhd,khd->hqk", grad_part, value_block, preferred_element_type=jnp.float32
            )
            row_dot = jnp.sum(probability * upstream, axis=2, keepdims=True)
            score_grad = (probability * (upstream - row_dot)).astype(jnp.bfloat16)
            rounded = probability.astype(jnp.bfloat16)
            key_total = totals[0] + jnp.einsum(
                "hqk,qhd->khd", score_grad, query_part, preferred_element_type=jnp.float32
            )
            value_total = totals[1] + jnp.einsum(
                "hqk,qhd->khd", rounded, grad_part, preferred_element_type=jnp.float32
            )
            totals = (key_total, value_total)
            query_grad = jnp.einsum(
                "hqk,khd->qhd", score_grad, key_block, preferred_element_type=jnp.float32
            ).astype(jnp.bfloat16)
            return (totals, query_grad.reshape(row_count, column_count))

        zeros = jnp.zeros((key_count, group_size, HEAD_DIM), jnp.float32)
        totals, query_grads = lax.scan(
            query_block, (zeros, zeros), jnp.arange(length // row_count, dtype=jnp.int32)
        )
        results = ()
        results = results + (query_grads.reshape(length, column_count),)
        results = results + (
            totals[0].reshape(key_count, column_count),
            totals[1].reshape(key_count, column_count),
        )
        return results

    pieces = lax.map(head_group, jnp.arange(head_count // group_size, dtype=jnp.int32))
    return tuple(
        (jnp.moveaxis(piece, 0, 1).reshape(piece.shape[1], full_width) for piece in pieces)
    )


def body(queries, out_grad, enc_states, w_key, w_value, dec_segments, enc_segments):
    encoder, key_ids = (
        lax.all_gather(enc_states, "ctx", axis=0, tiled=True),
        lax.all_gather(enc_segments, "ctx", axis=0, tiled=True),
    )
    key_weight, value_weight = side_by_side((w_key, w_value), "dp", 0, 1)
    key_part = jnp.dot(encoder, key_weight, preferred_element_type=jnp.float32).astype(jnp.bfloat16)
    value_part = jnp.dot(encoder, value_weight, preferred_element_type=jnp.float32).astype(
        jnp.bfloat16
    )
    local_queries, local_grads = (
        lax.all_to_all(queries, "ctx", split_axis=1, concat_axis=0, tiled=True),
        lax.all_to_all(out_grad, "ctx", split_axis=1, concat_axis=0, tiled=True),
    )
    query_ids = gathered_copies(dec_segments, "ctx", 0)
    head_grad, key_grad, value_grad = attend(
        local_queries, local_grads, key_part, value_part, query_ids, key_ids
    )
    query_grad = lax.all_to_all(head_grad, "ctx", split_axis=0, concat_axis=1, tiled=True)
    key_round = key_grad.astype(jnp.bfloat16)
    value_round = value_grad.astype(jnp.bfloat16)
    across = (((1,), (1,)), ((), ()))
    partial_value = lax.dot_general(
        key_round, key_weight, across, preferred_element_type=jnp.float32
    )
    partial_value = partial_value + lax.dot_general(
        value_round, value_weight, across, preferred_element_type=jnp.float32
    )
    enc_grad = sum_at_owner(partial_value.astype(jnp.bfloat16), "ctx", 0).astype(jnp.bfloat16)
    down = (((0,), (0,)), ((), ()))
    key_term = lax.dot_general(encoder, key_round, down, preferred_element_type=jnp.float32)
    value_term = lax.dot_general(encoder, value_round, down, preferred_element_type=jnp.float32)
    w_key_grad, w_value_grad = tuple(
        (
            part.astype(jnp.float32)
            for part in in_one_piece(
                (key_term.astype(jnp.bfloat16), value_term.astype(jnp.bfloat16)), "dp", 0, 1
            )
        )
    )
    return (query_grad, enc_grad, w_key_grad, w_value_grad)


def solution(mesh):
    in_specs = (
        P(("dp", "ctx"), None),
        P(("dp", "ctx"), None),
        P(("dp", "ctx"), None),
        P("dp", "ctx"),
        P("dp", "ctx"),
        P(("dp", "ctx")),
        P(("dp", "ctx")),
    )
    out_specs = (P(("dp", "ctx"), None), P(("dp", "ctx"), None), P("dp", "ctx"), P("dp", "ctx"))
    return jax.shard_map(body, mesh=mesh, in_specs=in_specs, out_specs=out_specs, check_vma=False)
```

profile of v0, /device:TPU:8, one launch (start us, length us, event | category | flops | bytes accessed | tf_op | source)
XLA Modules:
  0.0 417.5 jit_solution(9430888007886917703)
XLA Ops:
  7.2 4.1 copy.68
  11.2 11.7 %all-to-all-start = ((bf16[128,32,256]{0,2,1:T(8,128)(2,1)}), bf16[128,32,256]{0,2,1:T(8,128)(2,1)S(1)}, u32[]{:S(2)}, u32[]{:S(2)}) async-start(bf16[128,32,256]{0,2,1:T(8,128)(2,1)} %bitcast.99), calls=%async_computation | async-start | bytes 4194304 | tf_op jit(solution)/shard_map/all_to_all | solution.py:137
  22.9 4.1 copy.70
  27.1 44.4 %all-to-all-done = bf16[128,32,256]{0,2,1:T(8,128)(2,1)S(1)} async-done(((bf16[128,32,256]{0,2,1:T(8,128)(2,1)}), bf16[128,32,256]{0,2,1:T(8,128)(2,1)S(1)}, u32[]{:S(2)}, u32[]{:S(2)}) %all-to-all-start) | async-done | bytes 2097184 | tf_op jit(solution)/shard_map/all_to_all | solution.py:137
  72.8 7.6 %all-to-all-start.2 = ((bf16[128,32,256]{0,2,1:T(8,128)(2,1)}), bf16[128,32,256]{0,2,1:T(8,128)(2,1)}, u32[]{:S(2)}, u32[]{:S(2)}) async-start(bf16[128,32,256]{0,2,1:T(8,128)(2,1)} %bitcast.97), calls=%async_computation.2 | async-start | bytes 4194304 | tf_op jit(solution)/shard_map/all_to_all | solution.py:138
  81.2 96.0 %all-gather = bf16[32,12,1024]{2,1,0:T(8,128)(2,1)S(1)} all-gather(bf16[1,12,1024]{2,1,0:T(8,128)(2,1)S(1)} %bitcast.108), channel_id=1, replica_groups=mesh['dp'=8,'ctx'=32] {'ctx'}, dimensions={0}, use_global_device_ids=true | all-gather | bytes 811008 | tf_op jit(solution)/shard_map/all_gather | solution.py:128
  179.1 17.7 %all-reduce = s32[384]{0:T(512)S(1)} all-reduce(s32[384]{0:T(512)S(1)} %dynamic-update-slice), channel_id=1, replica_groups=mesh['dp'=8,'ctx'=32] {'ctx'}, use_global_device_ids=true, to_apply=%add | all-reduce | flops 384 | bytes 3072
  199.0 10.4 %all-to-all-start.1 = ((s32[32,1,128]{2,1,0:T(1,128)}), s32[32,1,128]{2,1,0:T(1,128)}, u32[]{:S(2)}, u32[]{:S(2)}) async-start(s32[32,1,128]{2,1,0:T(1,128)} %broadcast_in_dim.41), calls=%async_computation.1 | async-start | bytes 32768 | tf_op jit(solution)/shard_map/all_to_all | solution.py:21
  212.4 3.3 copy.69
  215.7 4.1 copy.71
  219.8 62.6 %while.27 = (s32[]{:T(128)}, f32[384,2,128]{0,2,1:T(8,128)S(1)}, f32[384,2,128]{0,2,1:T(8,128)}, bf16[4,1024,256]{2,1,0:T(8,128)(2,1)}, s32[4]{0:T(128)S(1)}, /*...) while((s32[]{:T(128)}, f32[384,2,128]{0,2,1:T(8,128)S(1)}, ...), condition=%wide.region_4.5_spmd.clone, body=%wide.region_0.4_spmd.clone.sunk | while | flops 1017117056 | bytes 58062732 | solution.py:109
  226.1 2.5 fusion.69
  228.7 2.6 fusion.71
  241.6 2.5 fusion.69
  244.2 2.7 fusion.71
  257.3 2.5 fusion.69
  259.9 2.7 fusion.71
  273.0 2.5 fusion.69
  275.6 2.7 fusion.71
  285.6 36.9 %all_to_all.68 = bf16[32,12,1024]{2,1,0:T(8,128)(2,1)} all-to-all(bf16[32,12,1024]{2,1,0:T(8,128)(2,1)S(1)} %reshape.98), channel_id=1, replica_groups=mesh['dp'=8,'ctx'=32] {'ctx'}, dimensions={0} | all-to-all | bytes 1572864 | tf_op jit(solution)/shard_map/all_to_all | solution.py:45
  322.5 6.9 %all-to-all-start.3 = ((bf16[32,128,256]{2,1,0:T(8,128)(2,1)}), bf16[32,128,256]{2,1,0:T(8,128)(2,1)S(1)}, u32[]{:S(2)}, u32[]{:S(2)}) async-start(bf16[32,128,256]{2,1,0:T(8,128)(2,1)} %bitcast.102), calls=%async_computation.3 | async-start | bytes 4194304 | tf_op jit(solution)/shard_map/all_to_all | solution.py:144
  334.7 66.3 %reduce-scatter.4.cloned.1.call-done = bf16[128,512]{1,0:T(8,128)(2,1)} async-done(((bf16[1024,512]{1,0:T(8,128)(2,1)}), bf16[128,512]{1,0:T(8,128)(2,1)}) %reduce-scatter.4.cloned.1.call-update) | async-done | bytes 131088
  403.7 2.9 copy.76
  406.6 4.1 copy.77
  (154 shorter events, 58.2 us)
Async XLA Ops:
  11.2 60.2 %all-to-all-start = ((bf16[128,32,256]{0,2,1:T(8,128)(2,1)}), bf16[128,32,256]{0,2,1:T(8,128)(2,1)S(1)}, u32[]{:S(2)}, u32[]{:S(2)}) async-start(bf16[128,32,256]{0,2,1:T(8,128)(2,1)} %bitcast.99), calls=%async_computation | async-start | bytes 4194304 | tf_op jit(solution)/shard_map/all_to_all | solution.py:137
  71.4 9.0 %copy-start.11 = (bf16[128,256]{1,0:T(8,128)(2,1)S(1)}, bf16[128,256]{1,0:T(8,128)(2,1)}, u32[]{:S(2)}) copy-start(bf16[128,256]{1,0:T(8,128)(2,1)} %param.13) | copy-start | bytes 196612
  71.4 9.1 %copy-start.12 = (bf16[128,256]{1,0:T(8,128)(2,1)S(1)}, bf16[128,256]{1,0:T(8,128)(2,1)}, u32[]{:S(2)}) copy-start(bf16[128,256]{1,0:T(8,128)(2,1)} %param.12) | copy-start | bytes 196612
  71.4 9.8 %copy-start.13 = (bf16[12,1024]{1,0:T(8,128)(2,1)S(1)}, bf16[12,1024]{1,0:T(8,128)(2,1)}, u32[]{:S(2)}) copy-start(bf16[12,1024]{1,0:T(8,128)(2,1)} %param.11) | copy-start | bytes 73732
  72.8 125.6 %all-to-all-start.2 = ((bf16[128,32,256]{0,2,1:T(8,128)(2,1)}), bf16[128,32,256]{0,2,1:T(8,128)(2,1)}, u32[]{:S(2)}, u32[]{:S(2)}) async-start(bf16[128,32,256]{0,2,1:T(8,128)(2,1)} %bitcast.97), calls=%async_computation.2 | async-start | bytes 4194304 | tf_op jit(solution)/shard_map/all_to_all | solution.py:138
  80.4 97.1 %copy-start.16 = (u32[256]{0:T(256)S(1)}, u32[256]{0:T(256)}, u32[]{:S(2)}) copy-start(u32[256]{0:T(256)} %constant.64) | copy-start | bytes 3076
  80.4 98.4 %copy-start.15 = (s32[12]{0:T(128)S(1)}, s32[12]{0:T(128)}, u32[]{:S(2)}) copy-start(s32[12]{0:T(128)} %param.15) | copy-start | bytes 148
  80.4 116.4 %all-gather.3.cloned.1.call-start = ((), (), s32[]{:S(2)}) async-start(), calls=%async_computation.6 | async-start | bytes 1179648 | tf_op jit(solution)/shard_map/all_gather | solution.py:16
  81.2 117.1 %copy-start.14 = (s32[128]{0:T(128)S(1)}, s32[128]{0:T(128)}, u32[]{:S(2)}) copy-start(s32[128]{0:T(128)} %param.14) | copy-start | bytes 1540
  177.5 38.2 %copy-start.5 = (bf16[384,1024]{1,0:T(8,128)(2,1)}, bf16[384,1024]{1,0:T(8,128)(2,1)S(1)}, u32[]{:S(2)}) copy-start(bf16[384,1024]{1,0:T(8,128)(2,1)S(1)} %reshape.103) | copy-start | bytes 2359300
  199.0 20.8 %all-to-all-start.1 = ((s32[32,1,128]{2,1,0:T(1,128)}), s32[32,1,128]{2,1,0:T(1,128)}, u32[]{:S(2)}, u32[]{:S(2)}) async-start(s32[32,1,128]{2,1,0:T(1,128)} %broadcast_in_dim.41), calls=%async_computation.1 | async-start | bytes 32768 | tf_op jit(solution)/shard_map/all_to_all | solution.py:21
  219.8 6.3 %copy-start.2 = (bf16[4096,256]{1,0:T(8,128)(2,1)}, bf16[4096,256]{1,0:T(8,128)(2,1)S(1)}, u32[]{:S(2)}) copy-start(bf16[4096,256]{1,0:T(8,128)(2,1)S(1)} %get-tuple-element.377) | copy-start | bytes 6291460 | tf_op jit(solution)/shard_map/while/body/eval_jaxpr/while
  235.4 6.3 %copy-start.2 = (bf16[4096,256]{1,0:T(8,128)(2,1)}, bf16[4096,256]{1,0:T(8,128)(2,1)S(1)}, u32[]{:S(2)}) copy-start(bf16[4096,256]{1,0:T(8,128)(2,1)S(1)} %get-tuple-element.377) | copy-start | bytes 6291460 | tf_op jit(solution)/shard_map/while/body/eval_jaxpr/while
  244.2 2.7 copy-start.1
  244.2 2.7 copy-start.10
  251.0 6.3 %copy-start.2 = (bf16[4096,256]{1,0:T(8,128)(2,1)}, bf16[4096,256]{1,0:T(8,128)(2,1)S(1)}, u32[]{:S(2)}) copy-start(bf16[4096,256]{1,0:T(8,128)(2,1)S(1)} %get-tuple-element.377) | copy-start | bytes 6291460 | tf_op jit(solution)/shard_map/while/body/eval_jaxpr/while
  259.9 2.7 copy-start.1
  259.9 2.7 copy-start.10
  266.7 6.3 %copy-start.2 = (bf16[4096,256]{1,0:T(8,128)(2,1)}, bf16[4096,256]{1,0:T(8,128)(2,1)S(1)}, u32[]{:S(2)}) copy-start(bf16[4096,256]{1,0:T(8,128)(2,1)S(1)} %get-tuple-element.377) | copy-start | bytes 6291460 | tf_op jit(solution)/shard_map/while/body/eval_jaxpr/while
  275.5 2.7 copy-start.1
  275.6 2.7 copy-start.10
  322.5 7.0 %copy-start.6 = (bf16[384,1024]{1,0:T(8,128)(2,1)S(1)}, bf16[384,1024]{1,0:T(8,128)(2,1)}, u32[]{:S(2)}) copy-start(bf16[384,1024]{1,0:T(8,128)(2,1)} %copy-done.5) | copy-start | bytes 2359300
  322.5 81.2 %all-to-all-start.3 = ((bf16[32,128,256]{2,1,0:T(8,128)(2,1)}), bf16[32,128,256]{2,1,0:T(8,128)(2,1)S(1)}, u32[]{:S(2)}, u32[]{:S(2)}) async-start(bf16[32,128,256]{2,1,0:T(8,128)(2,1)} %bitcast.102), calls=%async_computation.3 | async-start | bytes 4194304 | tf_op jit(solution)/shard_map/all_to_all | solution.py:144
  329.5 71.6 %reduce-scatter.4.cloned.1.call-start = ((), (), s32[]{:S(2)}) async-start(), calls=%async_computation.7 | async-start | bytes 1179648
  (17 other events, 25.7 us)
Sparse Core Ops, SparseCore 0:
  83.6 70.4 all-gather.2
  334.0 66.9 reduce-scatter.3
where the time goes:
time: 419 us; the launch traced here: 417 us
  blocking collectives  151 us (36%)
  waiting for transfers between devices  111 us (26%)
  local copies, waits for them, and re-layouts  56.4 us (13%)
  starting transfers between devices  36.7 us (9%)
  matrix products  33.8 us (8%)
  between operations  15 us (4%)
  other arithmetic  11.1 us (3%)
    all_gather x1, blocking collectives, body(): lax.all_gather(enc_states, 'ctx', axis=0, tiled=True)  96 us
    unnamed x3, waiting for transfers between devices  66.4 us
    all_to_all x1, waiting for transfers between devices, body(): lax.all_to_all(queries, 'ctx', split_axis=1, concat_axis=0, tiled=True)  44.4 us
    all_to_all x1, blocking collectives, sum_at_owner(): lax.all_to_all(pieces, axis, split_axis=0, concat_axis=0, tiled=True)  36.9 us
    unnamed x35, local copies, waits for them, and re-layouts  19.7 us
    unnamed x1, blocking collectives  17.7 us
    all_to_all x1, starting transfers between devices, body(): lax.all_to_all(queries, 'ctx', split_axis=1, concat_axis=0, tiled=True)  11.7 us
    dot_general x4, matrix products, query_block(): jnp.einsum('hqk,qhd->khd', rounded, grad_part, preferred_element_type=jnp...  10.5 us
  transfers between devices with their start and end apart: 6, of which 2 were waited for; matrix products, arithmetic and copies ran while one was open for 6% of the time, Pallas kernels for 0%

commit v1 on v0

--- a/solution.py
+++ b/solution.py
@@ -125,7 +125,9 @@
 
 def body(queries, out_grad, enc_states, w_key, w_value, dec_segments, enc_segments):
     encoder, key_ids = (
-        lax.all_gather(enc_states, "ctx", axis=0, tiled=True),
+        jnp.concatenate(
+            lax.all_to_all(jnp.stack([enc_states] * lax.axis_size("ctx")), "ctx", 0, 0), axis=0
+        ),
         lax.all_gather(enc_segments, "ctx", axis=0, tiled=True),
     )
     key_weight, value_weight = side_by_side((w_key, w_value), "dp", 0, 1)

time: 419 us -> 406 us (0.969)
  blocking collectives: 151 us -> 106 us
  waiting for transfers between devices: 111 us -> 137 us
  starting transfers between devices: 36.7 us -> 41.1 us
    all_gather x1 -> x0, blocking collectives: 96 us -> none  [body(): lax.all_gather(enc_states, 'ctx', axis=0, tiled=True)]
    unnamed x1, blocking collectives: 17.7 us -> 69 us
    all_to_all x0 -> x1, waiting for transfers between devices: none -> 25.2 us  [body(): lax.all_to_all(jnp.stack([enc_states] * lax.axis_size('ctx')), 'ctx', 0, 0)]
    all_to_all x0 -> x1, starting transfers between devices: none -> 11.7 us  [body(): lax.all_to_all(jnp.stack([enc_states] * lax.axis_size('ctx')), 'ctx', 0, 0)]
    all_to_all x1, starting transfers between devices: 11.7 us -> 6.65 us  [body(): lax.all_to_all(queries, 'ctx', split_axis=1, concat_axis=0, tiled=True)]
    unnamed x35 -> x34, local copies, waits for them, and re-layouts: 19.7 us -> 17.8 us
  transfers between devices with their start and end apart: 6 -> 7, of which waited for: 2 -> 3; matrix products, arithmetic and copies ran while one was open for 6% -> 7% of each run, Pallas kernels for 0% -> 0%
where the time goes in v1:
time: 406 us; the launch traced here: 404 us
  waiting for transfers between devices  137 us (34%)
  blocking collectives  106 us (26%)
  local copies, waits for them, and re-layouts  56.5 us (14%)
  starting transfers between devices  41.1 us (10%)
  matrix products  34.1 us (8%)
  between operations  15 us (4%)
  other arithmetic  11 us (3%)
    unnamed x1, blocking collectives  69 us
    unnamed x3, waiting for transfers between devices  66.4 us
    all_to_all x1, waiting for transfers between devices, body(): lax.all_to_all(queries, 'ctx', split_axis=1, concat_axis=0, tiled=True)  45.5 us
    all_to_all x1, blocking collectives, sum_at_owner(): lax.all_to_all(pieces, axis, split_axis=0, concat_axis=0, tiled=True)  37.3 us
    all_to_all x1, waiting for transfers between devices, body(): lax.all_to_all(jnp.stack([enc_states] * lax.axis_size('ctx')), 'ctx', 0, 0)  25.2 us
    unnamed x34, local copies, waits for them, and re-layouts  17.8 us
    all_to_all x1, starting transfers between devices, body(): lax.all_to_all(jnp.stack([enc_states] * lax.axis_size('ctx')), 'ctx', 0, 0)  11.7 us
    dot_general x4, matrix products, query_block(): jnp.einsum('hqk,qhd->khd', rounded, grad_part, preferred_element_type=jnp...  10.5 us
  transfers between devices with their start and end apart: 7, of which 3 were waited for; matrix products, arithmetic and copies ran while one was open for 7% of the time, Pallas kernels for 0%

profile of v1, /device:TPU:8, one launch (start us, length us, event | category | flops | bytes accessed | tf_op | source)
XLA Modules:
  0.0 404.3 jit_solution(16161976742626323768)
XLA Ops:
  9.2 11.7 %all-to-all-start.2 = ((bf16[32,12,1024]{2,1,0:T(8,128)(2,1)}), bf16[32,12,1024]{2,1,0:T(8,128)(2,1)S(1)}, u32[]{:S(2)}, u32[]{:S(2)}) async-start(bf16[32,12,1024]{2,1,0:T(8,128)(2,1)} %stack.2), calls=%async_computation.2 | async-start | bytes 2097152 | tf_op jit(solution)/shard_map/all_to_all | solution.py:129
  23.4 25.2 %all-to-all-done.2 = bf16[32,12,1024]{2,1,0:T(8,128)(2,1)S(1)} async-done(((bf16[32,12,1024]{2,1,0:T(8,128)(2,1)}), bf16[32,12,1024]{2,1,0:T(8,128)(2,1)S(1)}, u32[]{:S(2)}, u32[]{:S(2)}) %all-to-all-start.2) | async-done | bytes 786464 | tf_op jit(solution)/shard_map/all_to_all | solution.py:129
  48.6 6.6 %all-to-all-start = ((bf16[128,32,256]{0,2,1:T(8,128)(2,1)}), bf16[128,32,256]{0,2,1:T(8,128)(2,1)S(1)}, u32[]{:S(2)}, u32[]{:S(2)}) async-start(bf16[128,32,256]{0,2,1:T(8,128)(2,1)} %bitcast.98), calls=%async_computation | async-start | bytes 4194304 | tf_op jit(solution)/shard_map/all_to_all | solution.py:139
  55.2 4.1 %copy.70 = bf16[128,8192]{0,1:T(8,128)(2,1)} copy(bf16[128,8192]{1,0:T(8,128)(2,1)} %param.10) | data formatting | bytes 4194304 | tf_op args[1]
  59.3 45.5 %all-to-all-done = bf16[128,32,256]{0,2,1:T(8,128)(2,1)S(1)} async-done(((bf16[128,32,256]{0,2,1:T(8,128)(2,1)}), bf16[128,32,256]{0,2,1:T(8,128)(2,1)S(1)}, u32[]{:S(2)}, u32[]{:S(2)}) %all-to-all-start) | async-done | bytes 2097184 | tf_op jit(solution)/shard_map/all_to_all | solution.py:139
  106.2 7.5 %all-to-all-start.3 = ((bf16[128,32,256]{0,2,1:T(8,128)(2,1)}), bf16[128,32,256]{0,2,1:T(8,128)(2,1)}, u32[]{:S(2)}, u32[]{:S(2)}) async-start(bf16[128,32,256]{0,2,1:T(8,128)(2,1)} %bitcast.96), calls=%async_computation.3 | async-start | bytes 4194304 | tf_op jit(solution)/shard_map/all_to_all | solution.py:140
  116.0 69.0 %all-reduce = s32[384]{0:T(512)S(1)} all-reduce(s32[384]{0:T(512)S(1)} %dynamic-update-slice), channel_id=1, replica_groups=mesh['dp'=8,'ctx'=32] {'ctx'}, use_global_device_ids=true, to_apply=%add | all-reduce | flops 384 | bytes 3072
  187.6 8.2 %all-to-all-start.1 = ((s32[32,1,128]{2,1,0:T(1,128)}), s32[32,1,128]{2,1,0:T(1,128)}, u32[]{:S(2)}, u32[]{:S(2)}) async-start(s32[32,1,128]{2,1,0:T(1,128)} %broadcast_in_dim.41), calls=%async_computation.1 | async-start | bytes 32768 | tf_op jit(solution)/shard_map/all_to_all | solution.py:21
  198.8 3.3 copy.69
  202.1 4.1 %copy.71 = bf16[128,32,256]{2,0,1:T(8,128)(2,1)} copy(bf16[128,32,256]{0,2,1:T(8,128)(2,1)} %all-to-all-done.3) | data formatting | bytes 4194304 | tf_op jit(solution)/shard_map/all_to_all | solution.py:140
  206.2 62.5 %while.27 = (s32[]{:T(128)}, f32[384,2,128]{0,2,1:T(8,128)S(1)}, f32[384,2,128]{0,2,1:T(8,128)}, bf16[4,1024,256]{2,1,0:T(8,128)(2,1)}, s32[4]{0:T(128)S(1)}, /*...) while((s32[]{:T(128)}, f32[384,2,128]{0,2,1:T(8,128)S(1)}, ...), condition=%wide.region_4.5_spmd.clone, body=%wide.region_0.4_spmd.clone.sunk | while | flops 1017117056 | bytes 58062732 | solution.py:109
  212.5 2.5 fusion.69
  215.0 2.5 fusion.71
  228.0 2.5 fusion.69
  230.6 2.7 fusion.71
  243.6 2.5 fusion.69
  246.2 2.7 fusion.71
  259.3 2.5 fusion.69
  261.9 2.7 fusion.71
  271.9 37.3 %all_to_all.73 = bf16[32,12,1024]{2,1,0:T(8,128)(2,1)} all-to-all(bf16[32,12,1024]{2,1,0:T(8,128)(2,1)S(1)} %reshape.106), channel_id=1, replica_groups=mesh['dp'=8,'ctx'=32] {'ctx'}, dimensions={0} | all-to-all | bytes 1572864 | tf_op jit(solution)/shard_map/all_to_all | solution.py:45
  309.1 7.1 %all-to-all-start.4 = ((bf16[32,128,256]{2,1,0:T(8,128)(2,1)}), bf16[32,128,256]{2,1,0:T(8,128)(2,1)S(1)}, u32[]{:S(2)}, u32[]{:S(2)}) async-start(bf16[32,128,256]{2,1,0:T(8,128)(2,1)} %bitcast.101), calls=%async_computation.4 | async-start | bytes 4194304 | tf_op jit(solution)/shard_map/all_to_all | solution.py:146
  321.5 66.4 %reduce-scatter.4.cloned.1.call-done = bf16[128,512]{1,0:T(8,128)(2,1)} async-done(((bf16[1024,512]{1,0:T(8,128)(2,1)}), bf16[128,512]{1,0:T(8,128)(2,1)}) %reduce-scatter.4.cloned.1.call-update) | async-done | bytes 131088
  390.5 2.9 copy.76
  393.4 4.1 %copy.77 = bf16[128,8192]{1,0:T(8,128)(2,1)} copy(bf16[128,8192]{0,1:T(8,128)(2,1)} %bitcast.99) | data formatting | bytes 4194304
  (156 shorter events, 62.7 us)
Async XLA Ops:
  7.2 13.7 %copy-start.9 = (bf16[128,8192]{1,0:T(8,128)(2,1)S(1)}, bf16[128,8192]{1,0:T(8,128)(2,1)}, u32[]{:S(2)}) copy-start(bf16[128,8192]{1,0:T(8,128)(2,1)} %param.9) | copy-start | bytes 6291460
  9.2 39.4 %all-to-all-start.2 = ((bf16[32,12,1024]{2,1,0:T(8,128)(2,1)}), bf16[32,12,1024]{2,1,0:T(8,128)(2,1)S(1)}, u32[]{:S(2)}, u32[]{:S(2)}) async-start(bf16[32,12,1024]{2,1,0:T(8,128)(2,1)} %stack.2), calls=%async_computation.2 | async-start | bytes 2097152 | tf_op jit(solution)/shard_map/all_to_all | solution.py:129
  48.6 56.2 %all-to-all-start = ((bf16[128,32,256]{0,2,1:T(8,128)(2,1)}), bf16[128,32,256]{0,2,1:T(8,128)(2,1)S(1)}, u32[]{:S(2)}, u32[]{:S(2)}) async-start(bf16[128,32,256]{0,2,1:T(8,128)(2,1)} %bitcast.98), calls=%async_computation | async-start | bytes 4194304 | tf_op jit(solution)/shard_map/all_to_all | solution.py:139
  104.8 8.9 %copy-start.12 = (bf16[128,256]{1,0:T(8,128)(2,1)S(1)}, bf16[128,256]{1,0:T(8,128)(2,1)}, u32[]{:S(2)}) copy-start(bf16[128,256]{1,0:T(8,128)(2,1)} %param.13) | copy-start | bytes 196612
  104.8 8.9 %copy-start.13 = (bf16[128,256]{1,0:T(8,128)(2,1)S(1)}, bf16[128,256]{1,0:T(8,128)(2,1)}, u32[]{:S(2)}) copy-start(bf16[128,256]{1,0:T(8,128)(2,1)} %param.12) | copy-start | bytes 196612
  104.8 9.6 %copy-start.16 = (u32[256]{0:T(256)S(1)}, u32[256]{0:T(256)}, u32[]{:S(2)}) copy-start(u32[256]{0:T(256)} %constant.64) | copy-start | bytes 3076
  104.8 10.9 %copy-start.15 = (s32[12]{0:T(128)S(1)}, s32[12]{0:T(128)}, u32[]{:S(2)}) copy-start(s32[12]{0:T(128)} %param.15) | copy-start | bytes 148
  106.2 80.8 %all-to-all-start.3 = ((bf16[128,32,256]{0,2,1:T(8,128)(2,1)}), bf16[128,32,256]{0,2,1:T(8,128)(2,1)}, u32[]{:S(2)}, u32[]{:S(2)}) async-start(bf16[128,32,256]{0,2,1:T(8,128)(2,1)} %bitcast.96), calls=%async_computation.3 | async-start | bytes 4194304 | tf_op jit(solution)/shard_map/all_to_all | solution.py:140
  113.6 73.4 %copy-start.14 = (s32[128]{0:T(128)S(1)}, s32[128]{0:T(128)}, u32[]{:S(2)}) copy-start(s32[128]{0:T(128)} %param.14) | copy-start | bytes 1540
  113.6 71.5 %all-gather.2.cloned.1.call-start = ((), (), s32[]{:S(2)}) async-start(), calls=%async_computation.7 | async-start | bytes 1179648 | tf_op jit(solution)/shard_map/all_gather | solution.py:16
  185.2 12.9 %copy-start.5 = (bf16[384,1024]{1,0:T(8,128)(2,1)}, bf16[384,1024]{1,0:T(8,128)(2,1)S(1)}, u32[]{:S(2)}) copy-start(bf16[384,1024]{1,0:T(8,128)(2,1)S(1)} %reshape.103) | copy-start | bytes 2359300
  187.6 18.6 %all-to-all-start.1 = ((s32[32,1,128]{2,1,0:T(1,128)}), s32[32,1,128]{2,1,0:T(1,128)}, u32[]{:S(2)}, u32[]{:S(2)}) async-start(s32[32,1,128]{2,1,0:T(1,128)} %broadcast_in_dim.41), calls=%async_computation.1 | async-start | bytes 32768 | tf_op jit(solution)/shard_map/all_to_all | solution.py:21
  206.2 6.3 %copy-start.2 = (bf16[4096,256]{1,0:T(8,128)(2,1)}, bf16[4096,256]{1,0:T(8,128)(2,1)S(1)}, u32[]{:S(2)}) copy-start(bf16[4096,256]{1,0:T(8,128)(2,1)S(1)} %get-tuple-element.377) | copy-start | bytes 6291460 | tf_op jit(solution)/shard_map/while/body/eval_jaxpr/while
  221.7 6.3 %copy-start.2 = (bf16[4096,256]{1,0:T(8,128)(2,1)}, bf16[4096,256]{1,0:T(8,128)(2,1)S(1)}, u32[]{:S(2)}) copy-start(bf16[4096,256]{1,0:T(8,128)(2,1)S(1)} %get-tuple-element.377) | copy-start | bytes 6291460 | tf_op jit(solution)/shard_map/while/body/eval_jaxpr/while
  230.5 2.7 copy-start.1
  230.6 2.7 copy-start.11
  237.4 6.3 %copy-start.2 = (bf16[4096,256]{1,0:T(8,128)(2,1)}, bf16[4096,256]{1,0:T(8,128)(2,1)S(1)}, u32[]{:S(2)}) copy-start(bf16[4096,256]{1,0:T(8,128)(2,1)S(1)} %get-tuple-element.377) | copy-start | bytes 6291460 | tf_op jit(solution)/shard_map/while/body/eval_jaxpr/while
  246.2 2.7 copy-start.1
  246.2 2.7 copy-start.11
  253.0 6.3 %copy-start.2 = (bf16[4096,256]{1,0:T(8,128)(2,1)}, bf16[4096,256]{1,0:T(8,128)(2,1)S(1)}, u32[]{:S(2)}) copy-start(bf16[4096,256]{1,0:T(8,128)(2,1)S(1)} %get-tuple-element.377) | copy-start | bytes 6291460 | tf_op jit(solution)/shard_map/while/body/eval_jaxpr/while
  261.8 2.7 copy-start.1
  309.1 7.1 %copy-start.6 = (bf16[384,1024]{1,0:T(8,128)(2,1)S(1)}, bf16[384,1024]{1,0:T(8,128)(2,1)}, u32[]{:S(2)}) copy-start(bf16[384,1024]{1,0:T(8,128)(2,1)} %copy-done.5) | copy-start | bytes 2359300
  309.1 81.4 %all-to-all-start.4 = ((bf16[32,128,256]{2,1,0:T(8,128)(2,1)}), bf16[32,128,256]{2,1,0:T(8,128)(2,1)S(1)}, u32[]{:S(2)}, u32[]{:S(2)}) async-start(bf16[32,128,256]{2,1,0:T(8,128)(2,1)} %bitcast.101), calls=%async_computation.4 | async-start | bytes 4194304 | tf_op jit(solution)/shard_map/all_to_all | solution.py:146
  316.2 71.6 %reduce-scatter.4.cloned.1.call-start = ((), (), s32[]{:S(2)}) async-start(), calls=%async_computation.8 | async-start | bytes 1179648
  (18 other events, 28.4 us)
Sparse Core Ops, SparseCore 0:
  116.8 68.1 all-gather.1
  320.7 67.0 reduce-scatter.3
